TPU v7x, 512 devices: a whole 4x8x8 slice. The times are simulated.
512 devices in a mesh: seq: 64 (over y, z_hi, core), head: 8 (over x, z_lo).
Axes of the slice: x: 4, y: 8, z: 8 (z_hi: 4, z_lo: 2; z = z_hi * 2 + z_lo), core: 2. Of those that a mesh axis runs over, the one named last changes fastest.
Arguments:
- query_rows: bfloat16 [16384, 3072], P(('seq', 'head')), may hold values from -16 to 16
- key_rows: bfloat16 [16384, 1024], P(('seq', 'head')), may hold values from -16 to 16
- value_rows: bfloat16 [16384, 1024], P(('seq', 'head')), may hold values from -6 to 6
- residual: bfloat16 [16384, 3072], P(('seq', 'head')), may hold values from -6 to 6
- out_weight: bfloat16 [3072, 3072], P('head'), may hold values from -0.109375 to 0.109375
- gate_table: float32 [64, 3072], replicated, may hold values from -4 to 4
- noise_steps: int32 [8], replicated, may hold values from 0 to 63
- segment_mask: int32 [8, 8], replicated, may hold values from 0 to 1, as said below
- segment_map: int32 [64], replicated, may hold values from 0 to 7, as said below
Outputs:
- layer_output: bfloat16 [16384, 3072], P(('seq', 'head'))
Inputs may be any that keep to these rules, and one draw needn't show every extreme that they name: `segment_mask`: ones on the diagonal, zeros above it. `segment_map`: each segment number stands in exactly 8 entries.
All inputs are finite; a program needn't handle non-finite values.
Results may differ from a plain program's by a relative error of at most 0.0095.
Values may be sent and summed in bfloat16 or wider, within the bound.
A program may use at most 64 MiB of HBM per device.

v0:
```python
import math

import jax
import jax.numpy as jnp
from jax import lax
from jax.sharding import PartitionSpec as P

Q_HEADS = 24
KV_HEADS = 8
HEAD_DIM = 128


NEG = -1e30


def lookup(source_table, position):
    matches = jnp.arange(source_table.shape[0], dtype=jnp.int32) == position
    shaped = matches.reshape((-1,) + (1,) * (source_table.ndim - 1))
    return jnp.sum(jnp.where(shaped, source_table, jnp.zeros_like(source_table)), axis=0)


def visible_keys(owners, segment_map, mask_row):
    places = jnp.arange(segment_map.shape[0], dtype=jnp.int32)
    segment_ids = jnp.sum(
        jnp.where(owners[:, None] == places[None, :], segment_map[None, :], 0), axis=1
    )
    labels = jnp.arange(mask_row.shape[0], dtype=jnp.int32)
    return (
        jnp.sum(jnp.where(segment_ids[:, None] == labels[None, :], mask_row[None, :], 0), axis=1)
        > 0
    )


def attend_block(state_now, grouped, key_blk, value_blk, visible):
    running_max, weight_sum, accumulated = state_now
    kv_local = grouped.shape[1]
    head_size = grouped.shape[3]
    keys_three = key_blk.reshape(key_blk.shape[0], kv_local, head_size)
    values_three = value_blk.reshape(value_blk.shape[0], kv_local, head_size)
    scores = jnp.einsum(
        "qcgd,kcd->cgqk", grouped, keys_three, preferred_element_type=jnp.float32
    ) * head_size ** (-0.5)
    scores = jnp.where(visible, scores, NEG)
    new_max = jnp.maximum(running_max, jnp.max(scores, axis=-1))
    weights = jnp.where(visible, jnp.exp(scores - new_max[..., None]), 0.0)
    factor = jnp.exp(running_max - new_max)
    weight_sum = weight_sum * factor + jnp.sum(weights, axis=-1)
    product = jnp.einsum(
        "cgqk,kcd->cgqd",
        weights.astype(jnp.bfloat16),
        values_three,
        preferred_element_type=jnp.float32,
    )
    accumulated = accumulated * factor[..., None] + product
    return (new_max, weight_sum, accumulated)


def sweep(state_now, grouped, key_part, value_part, visible, block_size):
    num_blocks = key_part.shape[0] // block_size
    stacked = (
        key_part.reshape(num_blocks, block_size, key_part.shape[1]),
        value_part.reshape(num_blocks, block_size, value_part.shape[1]),
        visible.reshape(num_blocks, block_size),
    )

    def scan_step(state_in, block_item):
        key_blk, value_blk, seen_blk = block_item
        state_out = attend_block(state_in, grouped, key_blk, value_blk, seen_blk)
        return (state_out, None)

    return lax.scan(scan_step, state_now, stacked)[0]


def per_device(
    query_rows,
    key_rows,
    value_rows,
    residual,
    out_weight,
    gate_table,
    noise_steps,
    segment_mask,
    segment_map,
):
    n_head = lax.axis_size("head")
    row_count = query_rows.shape[0]
    tok_dev = row_count * n_head
    group_size = Q_HEADS // KV_HEADS
    kv_local = KV_HEADS // n_head
    local_queries = lax.all_to_all(query_rows, "head", split_axis=1, concat_axis=0, tiled=True)
    grouped = local_queries.reshape(tok_dev, kv_local, group_size, HEAD_DIM)
    own_segment = lookup(segment_map, lax.axis_index("seq"))
    mask_row = lookup(segment_mask, own_segment)
    initial = (
        jnp.full((kv_local, group_size, tok_dev), NEG, jnp.float32),
        jnp.zeros((kv_local, group_size, tok_dev), jnp.float32),
        jnp.zeros((kv_local, group_size, tok_dev, HEAD_DIM), jnp.float32),
    )
    local_keys, local_values = (
        lax.all_to_all(key_rows, "head", split_axis=1, concat_axis=0, tiled=True),
        lax.all_to_all(value_rows, "head", split_axis=1, concat_axis=0, tiled=True),
    )
    key_piece = lax.all_gather(local_keys, "seq", axis=0, tiled=True)
    value_piece = lax.all_gather(local_values, "seq", axis=0, tiled=True)
    piece_rows = key_piece.shape[0]
    owners = jnp.arange(piece_rows, dtype=jnp.int32) // tok_dev
    visible = visible_keys(owners, segment_map, mask_row)
    block_size = math.gcd(piece_rows, 512)
    final = sweep(initial, grouped, key_piece, value_piece, visible, block_size)
    running_max, weight_sum, accumulated = final
    normalized = accumulated / weight_sum[..., None]
    attended = jnp.transpose(normalized, (2, 0, 1, 3)).reshape(tok_dev, -1).astype(jnp.bfloat16)
    projected = lax.psum_scatter(
        jnp.dot(attended, out_weight, preferred_element_type=jnp.float32).astype(jnp.bfloat16),
        "head",
        scatter_dimension=0,
        tiled=True,
    ).astype(jnp.float32)
    step_now = lookup(noise_steps, own_segment)
    gate_row = lookup(gate_table, step_now)
    return (residual.astype(jnp.float32) + gate_row[None, :] * projected).astype(jnp.bfloat16)


def solution(mesh):
    placed = (
        P(("seq", "head"), None),
        P(("seq", "head"), None),
        P(("seq", "head"), None),
        P(("seq", "head"), None),
        P("head", None),
        P(),
        P(),
        P(),
        P(),
    )
    return jax.shard_map(
        per_device, mesh=mesh, in_specs=placed, out_specs=P(("seq", "head"), None), check_vma=False
    )
```

profile of v0, /device:TPU:6, one launch (start us, length us, event | category | flops | bytes accessed | tf_op | source)
XLA Modules:
  0.0 418.5 jit_solution(7602301493291203064)
XLA Ops:
  7.5 13.2 %all_to_all.54 = bf16[32,8,128]{2,0,1:T(8,128)(2,1)} all-to-all(bf16[32,8,128]{2,0,1:T(8,128)(2,1)S(1)} %copy_bitcast_fusion.2), channel_id=1, replica_groups=mesh['seq'=64,'head'=8] {'head'}, dimensions={1} | all-to-all | bytes 131072 | tf_op jit(solution)/shard_map/all_to_all | solution.py:100
  21.7 9.4 %all_to_all.55 = bf16[32,8,128]{2,0,1:T(8,128)(2,1)} all-to-all(bf16[32,8,128]{2,0,1:T(8,128)(2,1)S(1)} %copy_bitcast_fusion.1), channel_id=1, replica_groups=mesh['seq'=64,'head'=8] {'head'}, dimensions={1} | all-to-all | bytes 131072 | tf_op jit(solution)/shard_map/all_to_all | solution.py:101
  32.7 5.4 %all-to-all-start.1 = ((bf16[32,8,384]{2,0,1:T(8,128)(2,1)}), bf16[32,8,384]{2,0,1:T(8,128)(2,1)S(1)}, u32[]{:S(2)}, u32[]{:S(2)}) async-start(bf16[32,8,384]{2,0,1:T(8,128)(2,1)} %bitcast.74), calls=%async_computation.1 | async-start | bytes 393216 | tf_op jit(solution)/shard_map/all_to_all | solution.py:90
  43.1 67.4 %all-gather.3.cloned.1.call-done = bf16[16384,128]{1,0:T(8,128)(2,1)} async-done(((bf16[256,128]{1,0:T(8,128)(2,1)}), bf16[16384,128]{1,0:T(8,128)(2,1)}) %all-gather.3.cloned.1.call-update) | async-done | bytes 4194320 | tf_op jit(solution)/shard_map/all_gather | solution.py:103
  110.5 87.2 %all-gather.5.cloned.1.call-done = bf16[16384,128]{1,0:T(8,128)(2,1)} async-done(((bf16[256,128]{1,0:T(8,128)(2,1)}), bf16[16384,128]{1,0:T(8,128)(2,1)}) %all-gather.5.cloned.1.call-update) | async-done | bytes 4194320 | tf_op jit(solution)/shard_map/all_gather | solution.py:104
  197.7 166.1 %while.15 = (s32[]{:T(128)}, f32[1,3,256]{2,1,0:T(4,128)S(1)}, f32[1,3,256]{2,1,0:T(4,128)S(1)}, f32[1,3,256,128]{3,2,1,0:T(8,128)S(1)}, pred[32,512]{1,0:T(8,12...) while((s32[]{:T(128)}, f32[1,3,256]{2,1,0:T(4,128)S(1)}, ...), condition=%wide.region_9.10_spmd.clone, body=%wide.region_6.9_spmd.clone.sunk | while | flops 205165056 | bytes 12308113 | solution.py:71
  202.9 2.5 bitcast_reduce_fusion.2
  208.1 2.5 bitcast_reduce_fusion.2
  213.3 2.5 bitcast_reduce_fusion.2
  223.7 2.5 bitcast_reduce_fusion.2
  234.0 2.5 bitcast_reduce_fusion.2
  244.4 2.5 bitcast_reduce_fusion.2
  254.8 2.5 bitcast_reduce_fusion.2
  265.2 2.5 bitcast_reduce_fusion.2
  275.6 2.5 bitcast_reduce_fusion.2
  286.0 2.5 bitcast_reduce_fusion.2
  296.3 2.5 bitcast_reduce_fusion.2
  306.7 2.5 bitcast_reduce_fusion.2
  317.1 2.5 bitcast_reduce_fusion.2
  327.5 2.5 bitcast_reduce_fusion.2
  337.9 2.5 bitcast_reduce_fusion.2
  348.3 2.5 bitcast_reduce_fusion.2
  358.6 2.5 bitcast_reduce_fusion.2
  368.8 41.5 %reduce-scatter.2.cloned.1.call-done = bf16[32,3072]{1,0:T(8,128)(2,1)} async-done(((bf16[256,3072]{1,0:T(8,128)(2,1)}), bf16[32,3072]{1,0:T(8,128)(2,1)}) %reduce-scatter.2.cloned.1.call-update) | async-done | bytes 196624 | tf_op jit(solution)/shard_map/reduce_scatter | solution.py:113
  (309 shorter events, 137.0 us)
Async XLA Ops:
  6.5 357.5 %copy-start = (bf16[384,3072]{1,0:T(8,128)(2,1)S(1)}, bf16[384,3072]{1,0:T(8,128)(2,1)}, u32[]{:S(2)}) copy-start(bf16[384,3072]{1,0:T(8,128)(2,1)} %param.15) | copy-start | bytes 7077892
  6.5 103.9 %all-gather.3.cloned.1.call-start = ((), (), s32[]{:S(2)}) async-start(), calls=%async_computation.4 | async-start | bytes 4259840 | tf_op jit(solution)/shard_map/all_gather | solution.py:103
  20.7 176.9 %all-gather.5.cloned.1.call-start = ((), (), s32[]{:S(2)}) async-start(), calls=%async_computation.5 | async-start | bytes 4259840 | tf_op jit(solution)/shard_map/all_gather | solution.py:104
  32.7 10.3 %all-to-all-start.1 = ((bf16[32,8,384]{2,0,1:T(8,128)(2,1)}), bf16[32,8,384]{2,0,1:T(8,128)(2,1)S(1)}, u32[]{:S(2)}, u32[]{:S(2)}) async-start(bf16[32,8,384]{2,0,1:T(8,128)(2,1)} %bitcast.74), calls=%async_computation.1 | async-start | bytes 393216 | tf_op jit(solution)/shard_map/all_to_all | solution.py:90
  38.1 372.2 %reduce-scatter.2.cloned.1.call-start = ((), (), s32[]{:S(2)}) async-start(), calls=%async_computation.6 | async-start | bytes 1769472 | tf_op jit(solution)/shard_map/reduce_scatter | solution.py:113
  200.2 2.3 copy-start.1
  205.4 2.3 copy-start.1
  215.8 2.3 copy-start.1
  226.2 2.3 copy-start.1
  236.6 2.3 copy-start.1
  247.0 2.3 copy-start.1
  257.3 2.3 copy-start.1
  267.7 2.3 copy-start.1
  278.1 2.3 copy-start.1
  288.5 2.3 copy-start.1
  298.9 2.3 copy-start.1
  309.2 2.3 copy-start.1
  319.6 2.3 copy-start.1
  330.0 2.3 copy-start.1
  340.4 2.3 copy-start.1
  350.8 2.3 copy-start.1
  361.2 2.3 copy-start.1
  366.2 2.5 copy-start.2
  366.2 44.1 %copy-start.3 = (bf16[32,3072]{1,0:T(8,128)(2,1)S(1)}, bf16[32,3072]{1,0:T(8,128)(2,1)}, u32[]{:S(2)}) copy-start(bf16[32,3072]{1,0:T(8,128)(2,1)} %param.14) | copy-start | bytes 589828
  (16 other events, 34.9 us)
Sparse Core Ops, SparseCore 0:
  20.9 89.5 all-gather.2
  113.8 83.8 all-gather.4
  366.3 43.9 reduce-scatter.1
where the time goes:
time: 421 us; the launch traced here: 418 us
  waiting for transfers between devices  197 us (47%)
  matrix products  155 us (37%)
  blocking collectives  22.6 us (5%)
  other arithmetic  18.6 us (4%)
  between operations  13.2 us (3%)
  local copies, waits for them, and re-layouts  5.5 us (1%)
  starting transfers between devices  5.45 us (1%)
    all_gather x1, waiting for transfers between devices, per_device(): value_piece = lax.all_gather(local_values, 'seq', axis=0, tiled=True)  87.2 us
    dot_general x32, matrix products, attend_block(): jnp.einsum('qcgd,kcd->cgqk', grouped, keys_three, preferred_element_type=...  80.8 us
    dot_general x32, matrix products, attend_block(): jnp.einsum('cgqk,kcd->cgqd', weights.astype(jnp.bfloat16), values_three,...  72.3 us
    all_gather x1, waiting for transfers between devices, per_device(): key_piece = lax.all_gather(local_keys, 'seq', axis=0, tiled=True)  67.4 us
    reduce_scatter x1, waiting for transfers between devices, per_device(): lax.psum_scatter(jnp.dot(attended, out_weight, preferred_element_type=jnp...  41.5 us
    all_to_all x1, blocking collectives, per_device(): lax.all_to_all(key_rows, 'head', split_axis=1, concat_axis=0, tiled=True)  13.2 us
    reduce_sum x32, other arithmetic, attend_block(): weight_sum = weight_sum * factor + jnp.sum(weights, axis=-1)  9.72 us
    all_to_all x1, blocking collectives, per_device(): lax.all_to_all(value_rows, 'head', split_axis=1, concat_axis=0, tiled=True)  9.4 us
  transfers between devices with their start and end apart: 4, of which 4 were waited for; matrix products, arithmetic and copies ran while one was open for 2% of the time, Pallas kernels for 0%

commit v1 on v0

v1 whole, which is shorter than its diff:
```python
import functools

import jax
import jax.numpy as jnp
from jax import lax
from jax.experimental import pallas as pl
from jax.experimental.pallas import tpu as pltpu
from jax.sharding import PartitionSpec as P

HEAD_DIM = 128
GROUP = 3
GW = GROUP * HEAD_DIM
NZ = 4
NC = 2
MASKED = -1e30
FLOOR = -1e20
SCALE = 1.4426950408889634 / HEAD_DIM**0.5
MESH = pl.DeviceIdType.MESH
CHUNK = 1024


def nt_dot(a, b):
    return lax.dot_general(a, b, (((1,), (1,)), ((), ())), preferred_element_type=jnp.float32)


def kernel(
    ny, nh, rows,
    q_hbm, k_hbm, v_hbm, res_hbm, w_hbm, gate_hbm, steps_ref, mask_ref, map_ref,
    out_ref,
    kv, q_all, scores, mx_acc, mx, acc, stat, stat_send, stat_recv, o_own, o_send, o_recv,
    attended, w_v, gate_v, res_v, part, part_recv, bias,
    k_ss, k_rs, v_ss, v_rs, q_ss, q_rs, right_ss, right_rs, left_ss, left_rs,
    sib_ss, sib_rs, o_ss, o_rs, st_ss, st_rs, p_ss, p_rs, loc,
):
    seq = lax.axis_index("seq")
    head = lax.axis_index("head")
    core = lax.rem(seq, NC)
    zh = lax.rem(seq // NC, NZ)
    y = seq // (NC * NZ)
    tok = rows * nh
    n_slots = 2 * ny

    def place(py, pz, pc):
        return (py * NZ + pz) * NC + pc

    def at_head(d):
        return lax.rem(head + d, nh)

    def at_z(d):
        return lax.rem(zh + d, NZ)

    def at_y(d):
        return lax.rem(y + d + ny, ny)

    def dev(s, h):
        return {"seq": s, "head": h}

    other = place(y, zh, 1 - core)
    right = place(at_y(1), zh, core)
    left = place(at_y(-1), zh, core)

    barrier = pltpu.get_barrier_semaphore()
    for dz in range(NZ):
        for dh in range(nh):
            if dz or dh:
                pl.semaphore_signal(
                    barrier, inc=1, device_id=dev(place(y, at_z(dz), core), at_head(dh)), device_id_type=MESH
                )
    for target in (other, right, left):
        pl.semaphore_signal(barrier, inc=1, device_id=dev(target, head), device_id_type=MESH)

    def cols(h, width):
        return pl.ds(pl.multiple_of(h * width, HEAD_DIM), width)

    def own_rows(h):
        return pl.ds(pl.multiple_of(h * rows, rows), rows)

    local = [
        pltpu.make_async_copy(k_hbm.at[:, cols(head, HEAD_DIM)], kv.at[own_rows(head), 0:128], loc.at[0]),
        pltpu.make_async_copy(v_hbm.at[:, cols(head, HEAD_DIM)], kv.at[own_rows(head), 128:256], loc.at[1]),
        pltpu.make_async_copy(q_hbm.at[:, cols(head, GW)], q_all.at[0, own_rows(head)], loc.at[2]),
        pltpu.make_async_copy(w_hbm, w_v, loc.at[3]),
        pltpu.make_async_copy(gate_hbm, gate_v, loc.at[4]),
        pltpu.make_async_copy(res_hbm, res_v, loc.at[5]),
    ]
    for cp in local[:3]:
        cp.start()

    def fill(i, carry):
        d = i // n_slots
        j = lax.rem(i, n_slots)
        q_seg = map_ref[place(y, at_z(d), core)]
        k_seg = map_ref[place(at_y(j // 2), zh, lax.rem(core + j, 2))]
        bias[i] = jnp.where(mask_ref[q_seg, k_seg] > 0, 0.0, MASKED).astype(jnp.float32)
        return carry

    lax.fori_loop(0, NZ * n_slots, fill, 0)

    pl.semaphore_wait(barrier, NZ * nh - 1 + 3)

    sends = []

    def remote(src, dst, ss, rs, target):
        cp = pltpu.make_async_remote_copy(
            src_ref=src, dst_ref=dst, send_sem=ss, recv_sem=rs, device_id=target, device_id_type=MESH
        )
        cp.start()
        sends.append(cp)
        return cp

    kv_in = []
    for d in range(1, nh):
        target = dev(seq, at_head(d))
        kv_in.append(remote(k_hbm.at[:, cols(at_head(d), HEAD_DIM)], kv.at[own_rows(head), 0:128],
                            k_ss.at[d], k_rs.at[d], target))
        kv_in.append(remote(v_hbm.at[:, cols(at_head(d), HEAD_DIM)], kv.at[own_rows(head), 128:256],
                            v_ss.at[d], v_rs.at[d], target))
    q_in = {s: [] for s in range(NZ)}
    for dz in (0, 1, 3, 2):
        if dz >= NZ:
            continue
        slot = (NZ - dz) % NZ
        for dh in range(nh):
            if dz or dh:
                i = dz * nh + dh
                q_in[slot].append(remote(q_hbm.at[:, cols(at_head(dh), GW)], q_all.at[slot, own_rows(head)],
                                         q_ss.at[i], q_rs.at[i], dev(place(y, at_z(dz), core), at_head(dh))))
    for cp in local[3:]:
        cp.start()

    def ones(i, carry):
        kv[pl.ds(pl.multiple_of(i * 256, 256), 256), 256:384] = jnp.ones((256, 128), jnp.bfloat16)
        return carry

    lax.fori_loop(0, n_slots * tok // 256, ones, 0)

    local[0].wait()
    local[1].wait()
    for cp in kv_in:
        cp.wait_recv()

    def block(r, c, lo=0, hi=256):
        return kv.at[pl.ds((r * 2 + c) * tok, tok), lo:hi]

    half = ny // 2
    sib = []

    def pass_on(r):
        sib.append(remote(block(r, 0), block(r, 1), sib_ss.at[r], sib_rs.at[r], dev(other, head)))

    r_in = l_in = None
    for s in range(half + 1):
        if s:
            r_in.wait_recv()
            l_in.wait_recv()
        if s < half:
            lo, hi = (0, 256) if s < half - 1 else (0, 128)
            lo2, hi2 = (0, 256) if s < half - 1 else (128, 256)
            r_in = remote(block((ny - s) % ny, 0, lo, hi), block((ny - s - 1) % ny, 0, lo, hi),
                          right_ss.at[s], right_rs.at[s], dev(right, head))
            l_in = remote(block(s, 0, lo2, hi2), block(s + 1, 0, lo2, hi2),
                          left_ss.at[s], left_rs.at[s], dev(left, head))
        pass_on(s)
        if 0 < s < half:
            pass_on(ny - s)
    for cp in sib:
        cp.wait_recv()
    local[2].wait()
    for cp in q_in[0]:
        cp.wait_recv()

    n_chunks = n_slots * tok // CHUNK if n_slots * tok >= CHUNK else 1
    width = n_slots * tok // n_chunks
    per = width // tok

    def key_rows_of(jc):
        return pl.ds(pl.multiple_of(jc * width, 128), width)

    def first(jc, q_tile, d, buf):
        s = nt_dot(q_tile, kv[key_rows_of(jc), 0:128])
        scores[buf, :, key_rows_of(jc)] = s
        m = mx_acc[...]
        for b in range(per):
            off = bias[d * n_slots + jc * per + b]
            for e in range(tok // 128):
                at = b * tok + e * 128
                m = jnp.maximum(m, s[:, at:at + 128] + off)
        mx_acc[...] = m

    def second(jc, d, buf):
        m = mx[...]
        pieces = []
        s = scores[buf, :, key_rows_of(jc)]
        for b in range(per):
            shift = (bias[d * n_slots + jc * per + b] - m) * SCALE
            for e in range(tok // 128):
                at = b * tok + e * 128
                pieces.append(jnp.exp2(s[:, at:at + 128] * SCALE + shift).astype(jnp.bfloat16))
        p = jnp.concatenate(pieces, axis=1)
        acc[...] += jnp.dot(p, kv[key_rows_of(jc), 128:384], preferred_element_type=jnp.float32)

    def close_first():
        mx[...] = jnp.broadcast_to(jnp.max(mx_acc[...], axis=1, keepdims=True), (tok, 128))
        mx_acc[...] = jnp.full((tok, 128), FLOOR, jnp.float32)
        acc[...] = jnp.zeros((tok, 256), jnp.float32)

    order = [s for s in (0, 1, 3, 2) if s < NZ]
    tiles = [(d, g) for d in order for g in range(GROUP)]
    lane = lax.broadcasted_iota(jnp.int32, (tok, 128), 1)

    mx_acc[...] = jnp.full((tok, 128), FLOOR, jnp.float32)

    def start_tile(d, g):
        return q_all[d, :, g * 128:(g + 1) * 128]

    q_tile = start_tile(*tiles[0])

    def only_first(jc, carry):
        first(jc, q_tile, tiles[0][0], 0)
        return carry

    lax.fori_loop(0, n_chunks, only_first, 0)
    close_first()
    o_in = {}
    for t, (d, g) in enumerate(tiles):
        buf = t % 2
        more = t + 1 < len(tiles)
        if more:
            nd, ng = tiles[t + 1]
            if ng == 0:
                for cp in q_in[nd]:
                    cp.wait_recv()
            q_next = start_tile(nd, ng)

        def both(jc, carry):
            second(jc, d, buf)
            if more:
                first(jc, q_next, nd, 1 - buf)
            return carry

        lax.fori_loop(0, n_chunks, both, 0)
        total = jnp.maximum(acc[:, 128:256], 1e-30)
        value = acc[:, 0:128] / total
        level = mx[...] * SCALE + jnp.log2(total)
        stat[...] = jnp.where(lane == g, level, stat[...]) if g else level
        if d == 0:
            o_own[:, g * 128:(g + 1) * 128] = value
        else:
            o_send[d - 1, :, g * 128:(g + 1) * 128] = value.astype(jnp.bfloat16)
        if g == GROUP - 1:
            if d == 0:
                stat_recv[0] = jnp.transpose(stat[...])[0:8]
            else:
                slot = (NZ - d) % NZ
                stat_send[d - 1] = jnp.transpose(stat[...])[0:8]
                target = dev(place(y, at_z(d), core), head)
                o_in[slot] = (
                    remote(o_send.at[d - 1], o_recv.at[slot - 1], o_ss.at[d - 1], o_rs.at[d - 1], target),
                    remote(stat_send.at[d - 1], stat_recv.at[slot], st_ss.at[d - 1], st_rs.at[d - 1], target),
                )
        if more:
            close_first()

    for slot in o_in:
        for cp in o_in[slot]:
            cp.wait_recv()
    zeros = jnp.zeros((120, tok), jnp.float32)
    levels = [jnp.transpose(jnp.concatenate([stat_recv[i], zeros], axis=0)) for i in range(NZ)]
    top = functools.reduce(jnp.maximum, levels)
    shares = [jnp.exp2(v - top) for v in levels]
    whole = functools.reduce(jnp.add, shares)
    shares = [v / whole for v in shares]
    for g in range(GROUP):
        at = slice(g * 128, (g + 1) * 128)
        mixed = shares[0][:, g:g + 1] * o_own[:, at]
        for i in range(1, NZ):
            mixed += shares[i][:, g:g + 1] * o_recv[i - 1, :, at].astype(jnp.float32)
        attended[:, at] = mixed.astype(jnp.bfloat16)

    local[3].wait()
    n_cols = w_v.shape[1]
    width_p = min(CHUNK, n_cols)
    p_in = []
    for ci in range(n_cols // width_p):
        at = slice(ci * width_p, (ci + 1) * width_p)
        part[:, at] = jnp.dot(attended[...], w_v[:, at], preferred_element_type=jnp.float32).astype(jnp.bfloat16)
        row = []
        for d in range(1, nh):
            to = at_head(d)
            row.append(remote(part.at[own_rows(to), at], part_recv.at[d - 1, :, at],
                              p_ss.at[ci * nh + d], p_rs.at[ci * nh + d], dev(seq, to)))
        p_in.append(row)
    local[4].wait()
    local[5].wait()
    step = steps_ref[map_ref[seq]]
    for ci in range(n_cols // width_p):
        at = slice(ci * width_p, (ci + 1) * width_p)
        for cp in p_in[ci]:
            cp.wait_recv()
        summed = part[own_rows(head), at].astype(jnp.float32)
        for d in range(1, nh):
            summed += part_recv[d - 1, :, at].astype(jnp.float32)
        gate = gate_v[pl.ds(step, 1), at]
        out_ref[:, at] = (res_v[:, at].astype(jnp.float32) + gate * summed).astype(out_ref.dtype)
    for cp in sends:
        cp.wait_send()


def per_device(ny, nh, query, key, value, residual, out_weight, gate_table, noise_steps, segment_mask, segment_map):
    rows, n_cols = query.shape
    tok = rows * nh
    n_keys = 2 * ny * tok
    bf, f32 = jnp.bfloat16, jnp.float32
    dma = lambda n: pltpu.SemaphoreType.DMA((n,))
    n_p = max(1, n_cols // CHUNK) * nh
    hbm = pl.BlockSpec(memory_space=pl.ANY)
    smem = pl.BlockSpec(memory_space=pltpu.SMEM)
    return pl.pallas_call(
        functools.partial(kernel, ny, nh, rows),
        out_shape=jax.ShapeDtypeStruct(residual.shape, residual.dtype),
        in_specs=[hbm] * 6 + [smem] * 3,
        out_specs=pl.BlockSpec(memory_space=pltpu.VMEM),
        scratch_shapes=[
            pltpu.VMEM((n_keys, 384), bf),
            pltpu.VMEM((NZ, tok, GW), bf),
            pltpu.VMEM((2, tok, n_keys), f32),
            pltpu.VMEM((tok, 128), f32),
            pltpu.VMEM((tok, 128), f32),
            pltpu.VMEM((tok, 256), f32),
            pltpu.VMEM((tok, 128), f32),
            pltpu.VMEM((NZ - 1, 8, tok), f32),
            pltpu.VMEM((NZ, 8, tok), f32),
            pltpu.VMEM((tok, GW), f32),
            pltpu.VMEM((NZ - 1, tok, GW), bf),
            pltpu.VMEM((NZ - 1, tok, GW), bf),
            pltpu.VMEM((tok, GW), bf),
            pltpu.VMEM(out_weight.shape, bf),
            pltpu.VMEM(gate_table.shape, f32),
            pltpu.VMEM(residual.shape, bf),
            pltpu.VMEM((tok, n_cols), bf),
            pltpu.VMEM((nh - 1, rows, n_cols), bf),
            pltpu.SMEM((NZ * 2 * ny,), f32),
            dma(nh), dma(nh), dma(nh), dma(nh), dma(NZ * nh), dma(NZ * nh),
            dma(ny), dma(ny), dma(ny), dma(ny), dma(ny), dma(ny),
            dma(NZ), dma(NZ), dma(NZ), dma(NZ), dma(n_p), dma(n_p), dma(6),
        ],
        compiler_params=pltpu.CompilerParams(
            collective_id=0, has_side_effects=True, vmem_limit_bytes=56 * 2**20
        ),
        name="segment_attention",
    )(query, key, value, residual, out_weight, gate_table, noise_steps, segment_mask, segment_map)


def solution(mesh):
    nh = mesh.shape["head"]
    ny = mesh.shape["seq"] // (NZ * NC)
    rows = P(("seq", "head"), None)
    return jax.shard_map(
        functools.partial(per_device, ny, nh),
        mesh=mesh,
        in_specs=(rows, rows, rows, rows, P("head", None), P(), P(), P(), P()),
        out_specs=rows,
        check_vma=False,
    )
```

time: 421 us -> 105 us (0.25)
  waiting for transfers between devices: 197 us -> 0 us
  matrix products: 155 us -> 0 us
  Pallas kernels: 0 us -> 103 us
  blocking collectives: 22.6 us -> 0 us
  other arithmetic: 18.6 us -> 0 us
  between operations: 13.2 us -> 0.01 us
  starting transfers between devices: 5.45 us -> 0 us
    dot_general x65 -> x0, matrix products: 155 us -> none  [the longest x32 80.8 us: attend_block(): jnp.einsum('qcgd,kcd->cgqk', grouped, keys_three, preferred_element_type=...]
    all_gather x2 -> x0, waiting for transfers between devices: 155 us -> none  [the longest x1 87.2 us: per_device(): value_piece = lax.all_gather(local_values, 'seq', axis=0, tiled=True)]
    pallas_call x0 -> x1, Pallas kernels: none -> 103 us  [per_device(): pl.pallas_call(functools.partial(kernel, ny, nh, rows), out_shape=jax.Sha...]
    reduce_scatter x1 -> x0, waiting for transfers between devices: 41.5 us -> none  [per_device(): lax.psum_scatter(jnp.dot(attended, out_weight, preferred_element_type=jnp...]
    all_to_all x2 -> x0, blocking collectives: 22.6 us -> none  [the longest x1 13.2 us: per_device(): lax.all_to_all(key_rows, 'head', split_axis=1, concat_axis=0, tiled=True)]
    reduce_sum x38 -> x0, other arithmetic: 14.8 us -> none  [the longest x32 9.72 us: attend_block(): weight_sum = weight_sum * factor + jnp.sum(weights, axis=-1)]
    all_to_all x1 -> x0, starting transfers between devices: 5.4 us -> none  [per_device(): lax.all_to_all(query_rows, 'head', split_axis=1, concat_axis=0, tiled=True)]
  transfers between devices with their start and end apart: 4 -> 0, of which waited for: 4 -> 0; matrix products, arithmetic and copies ran while one was open for 2% -> 0% of each run, Pallas kernels for 0% -> 0%
where the time goes in v1:
time: 105 us; the launch traced here: 104 us
  Pallas kernels  103 us (98%)
  local copies, waits for them, and re-layouts  1.62 us (2%)
    pallas_call x1, Pallas kernels, per_device(): pl.pallas_call(functools.partial(kernel, ny, nh, rows), out_shape=jax.Sha...  103 us

profile of v1, /device:TPU:6, one launch (start us, length us, event | category | flops | bytes accessed | tf_op | source)
XLA Modules:
  0.0 104.5 jit_solution(2254834066629900117)
XLA Ops:
  0.0 102.9 %segment_attention.1 = bf16[32,3072]{1,0:T(8,128)(2,1)} custom-call(bf16[32,3072]{1,0:T(8,128)(2,1)} %q_hbm.1, bf16[32,1024]{1,0:T(8,128)(2,1)} %k_hbm.1, bf16[32,1024]{1,0:T(8,128)(2,1)} %v_hbm.1, bf16[32,3072]{1,0:T(8,128)(2,1)} %res_hbm.1, bf16[384,3072]{1,0:T(8,128)(2,1)} %w_hbm.1, f32[64,3072]{1,0:T(8,128)} %gate_hbm.1, s32[8]{0:T(128)} %steps_ref.1, ...), custom_call_target="tpu_custom_call" | custom-call | tf_op jit(solution)/shard_map/segment_attention/pallas_call | solution.py:318
  102.9 1.6 %copy.11 = bf16[32,3072]{1,0:T(8,128)(2,1)} copy(bf16[32,3072]{1,0:T(8,128)(2,1)} %segment_attention.1) | data formatting | bytes 393216

commit v2 on v1

v2 whole, which is shorter than its diff:
```python
import functools

import jax
import jax.numpy as jnp
from jax import lax
from jax.experimental import pallas as pl
from jax.experimental.pallas import tpu as pltpu
from jax.sharding import PartitionSpec as P

HEAD_DIM = 128
GROUP = 3
GW = GROUP * HEAD_DIM
NZ = 4
NC = 2
NL = 2
HALVES = 2
MASKED = -1e30
FLOOR = -1e20
SCALE = 1.4426950408889634 / HEAD_DIM**0.5
MESH = pl.DeviceIdType.MESH
CHUNK = 1024


def nt_dot(a, b):
    return lax.dot_general(a, b, (((1,), (1,)), ((), ())), preferred_element_type=jnp.float32)


def kernel(
    ny, nh, rows,
    q_hbm, k_hbm, v_hbm, res_hbm, w_hbm, gate_hbm, steps_ref, mask_ref, map_ref,
    out_ref,
    kv, q_all, q_tile, scores, mx_acc, mx, acc, stat_send, stat_recv, o_own, o_send, o_recv,
    attended, w_v, gate_v, res_v, part, x_recv, summed, z_send, z_recv, bias,
    k_ss, k_rs, v_ss, v_rs, q_ss, q_rs, z_ss, z_rs, right_ss, right_rs, left_ss, left_rs,
    sib_ss, sib_rs, o_ss, o_rs, st_ss, st_rs, p_ss, p_rs, e_ss, e_rs, loc,
):
    seq = lax.axis_index("seq")
    head = lax.axis_index("head")
    core = lax.rem(seq, NC)
    zh = lax.rem(seq // NC, NZ)
    y = seq // (NC * NZ)
    nx = nh // NL
    x = head // NL
    zl = lax.rem(head, NL)
    tok = rows * nh
    part_rows = rows // HALVES
    tok_h = tok // HALVES
    n_slots = 2 * ny

    def place(py, pz, pc):
        return (py * NZ + pz) * NC + pc

    def at_head(d):
        return lax.rem(head + d, nh)

    def at_x(d):
        return lax.rem(x + d, nx)

    def at_z(d):
        return lax.rem(zh + d, NZ)

    def at_y(d):
        return lax.rem(y + d + ny, ny)

    def dev(s, h):
        return {"seq": s, "head": h}

    other = place(y, zh, 1 - core)
    right = place(at_y(1), zh, core)
    left = place(at_y(-1), zh, core)
    peers = [dev(seq, at_head(d)) for d in range(1, nh)]
    peers += [dev(place(y, at_z(d), core), head) for d in range(1, NZ)]
    peers += [dev(other, head), dev(right, head), dev(left, head)]

    barrier = pltpu.get_barrier_semaphore()
    for target in peers:
        pl.semaphore_signal(barrier, inc=1, device_id=target, device_id_type=MESH)

    def cols(h, width):
        return pl.ds(pl.multiple_of(h * width, HEAD_DIM), width)

    def own_rows(h, count):
        return pl.ds(pl.multiple_of(h * count, count), count)

    local = [
        pltpu.make_async_copy(k_hbm.at[:, cols(head, HEAD_DIM)], kv.at[own_rows(head, rows), 0:128], loc.at[0]),
        pltpu.make_async_copy(v_hbm.at[:, cols(head, HEAD_DIM)], kv.at[own_rows(head, rows), 128:256], loc.at[1]),
        pltpu.make_async_copy(q_hbm.at[:, :, cols(head, GW)], q_all.at[0, :, own_rows(head, part_rows)], loc.at[2]),
        pltpu.make_async_copy(w_hbm, w_v, loc.at[3]),
        pltpu.make_async_copy(gate_hbm, gate_v, loc.at[4]),
        pltpu.make_async_copy(res_hbm, res_v, loc.at[5]),
    ]
    for cp in local[:3]:
        cp.start()

    q_segs = [map_ref[place(y, at_z(d), core)] for d in range(NZ)]
    for j in range(n_slots):
        k_seg = map_ref[place(at_y(j // 2), zh, core if j % 2 == 0 else 1 - core)]
        for d in range(NZ):
            bias[d * n_slots + j] = jnp.where(mask_ref[q_segs[d], k_seg] > 0, 0.0, MASKED).astype(jnp.float32)

    pl.semaphore_wait(barrier, len(peers))

    sends = []

    def remote(src, dst, ss, rs, target):
        cp = pltpu.make_async_remote_copy(
            src_ref=src, dst_ref=dst, send_sem=ss, recv_sem=rs, device_id=target, device_id_type=MESH
        )
        cp.start()
        sends.append(cp)
        return cp

    kv_in, q_in = [], []
    for d in range(1, nh):
        target = dev(seq, at_head(d))
        kv_in.append(remote(k_hbm.at[:, cols(at_head(d), HEAD_DIM)], kv.at[own_rows(head, rows), 0:128],
                            k_ss.at[d], k_rs.at[d], target))
        kv_in.append(remote(v_hbm.at[:, cols(at_head(d), HEAD_DIM)], kv.at[own_rows(head, rows), 128:256],
                            v_ss.at[d], v_rs.at[d], target))
    for d in range(1, nh):
        q_in.append(remote(q_hbm.at[:, :, cols(at_head(d), GW)], q_all.at[0, :, own_rows(head, part_rows)],
                           q_ss.at[d], q_rs.at[d], dev(seq, at_head(d))))

    z_in = {}

    def send_queries():
        local[2].wait()
        for cp in q_in:
            cp.wait_recv()
        for hf in range(HALVES):
            for dz in (1, 3, 2):
                slot = NZ - dz
                i = hf * NZ + dz
                z_in[hf, slot] = remote(q_all.at[0, hf], q_all.at[slot, hf], z_ss.at[i], z_rs.at[i],
                                        dev(place(y, at_z(dz), core), head))
        for cp in local[3:]:
            cp.start()

    local[0].wait()
    local[1].wait()
    for cp in kv_in:
        cp.wait_recv()

    def block(r, c, lo=0, hi=256):
        return kv.at[pl.ds((r * 2 + c) * tok, tok), lo:hi]

    def ones(i, carry):
        kv[pl.ds(pl.multiple_of(i * 256, 256), 256), 256:384] = jnp.ones((256, 128), jnp.bfloat16)
        return carry

    half = ny // 2
    sib = []
    parts = ((0, 128), (128, 256))

    def pass_on(r, i):
        lo, hi = parts[i]
        sib.append(remote(block(r, 0, lo, hi), block(r, 1, lo, hi),
                          sib_ss.at[2 * r + i], sib_rs.at[2 * r + i], dev(other, head)))

    r_in, l_in = {}, {}
    for s in range(half + 1):
        for i in range(2):
            lo, hi = parts[i]
            if s and i in r_in:
                r_in.pop(i).wait_recv()
            if s < half - 1 or (s == half - 1 and i == 0):
                r_in[i] = remote(block((ny - s) % ny, 0, lo, hi), block((ny - s - 1) % ny, 0, lo, hi),
                                 right_ss.at[2 * s + i], right_rs.at[2 * s + i], dev(right, head))
            if s and i in l_in:
                l_in.pop(i).wait_recv()
            if s < half - 1 or (s == half - 1 and i == 1):
                l_in[i] = remote(block(s, 0, lo, hi), block(s + 1, 0, lo, hi),
                                 left_ss.at[2 * s + i], left_rs.at[2 * s + i], dev(left, head))
            pass_on(s, i)
            if 0 < s < half:
                pass_on(ny - s, i)
        if s == 0:
            send_queries()
            lax.fori_loop(0, n_slots * tok // 256, ones, 0)
    for cp in sib:
        cp.wait_recv()

    n_chunks = n_slots * tok // CHUNK
    per = CHUNK // tok
    rows_t = GROUP * tok_h

    def key_rows_of(jc):
        return pl.ds(pl.multiple_of(jc * CHUNK, CHUNK), CHUNK)

    def first(jc, d, buf):
        s = nt_dot(q_tile[buf], kv[key_rows_of(jc), 0:128])
        scores[buf, :, key_rows_of(jc)] = s
        m = mx_acc[...]
        for b in range(per):
            off = bias[d * n_slots + jc * per + b]
            for e in range(tok // 128):
                at = b * tok + e * 128
                m = jnp.maximum(m, s[:, at:at + 128] + off)
        mx_acc[...] = m

    def second(jc, d, buf):
        m = mx[...]
        pieces = []
        s = scores[buf, :, key_rows_of(jc)]
        for b in range(per):
            shift = (bias[d * n_slots + jc * per + b] - m) * SCALE
            for e in range(tok // 128):
                at = b * tok + e * 128
                pieces.append(jnp.exp2(s[:, at:at + 128] * SCALE + shift).astype(jnp.bfloat16))
        p = jnp.concatenate(pieces, axis=1)
        acc[...] += jnp.dot(p, kv[key_rows_of(jc), 128:384], preferred_element_type=jnp.float32)

    def close_first():
        mx[...] = jnp.broadcast_to(jnp.max(mx_acc[...], axis=1, keepdims=True), (rows_t, 128))
        mx_acc[...] = jnp.full((rows_t, 128), FLOOR, jnp.float32)
        acc[...] = jnp.zeros((rows_t, 256), jnp.float32)

    tiles = [(0, d) for d in (0, 1, 3, 2)] + [(1, d) for d in (1, 3, 2, 0)]
    lane = lax.broadcasted_iota(jnp.int32, (tok_h, 128), 1)

    mx_acc[...] = jnp.full((rows_t, 128), FLOOR, jnp.float32)

    def load_tile(t):
        hf, d = tiles[t]
        if d:
            z_in[hf, d].wait_recv()
        for g in range(GROUP):
            q_tile[t % 2, g * tok_h:(g + 1) * tok_h] = q_all[d, hf, :, g * 128:(g + 1) * 128]

    n_cols = w_v.shape[1]
    o_in, p_in, e_in = {}, {}, {}

    def close_second(hf, d):
        total = jnp.maximum(acc[:, 128:256], 1e-30)
        value = acc[:, 0:128] / total
        level = mx[...] * SCALE + jnp.log2(total)
        stat = level[0:tok_h]
        for g in range(1, GROUP):
            stat = jnp.where(lane == g, level[g * tok_h:(g + 1) * tok_h], stat)
        stat = jnp.transpose(stat)[0:8]
        for g in range(GROUP):
            piece = value[g * tok_h:(g + 1) * tok_h]
            if d == 0:
                o_own[hf, :, g * 128:(g + 1) * 128] = piece
            else:
                o_send[hf, d - 1, :, g * 128:(g + 1) * 128] = piece.astype(jnp.bfloat16)
        if d == 0:
            stat_recv[hf, 0] = stat
            return
        slot = NZ - d
        stat_send[hf, d - 1] = stat
        target = dev(place(y, at_z(d), core), head)
        i = hf * NZ + d
        o_in[hf, slot] = (
            remote(o_send.at[hf, d - 1], o_recv.at[hf, slot - 1], o_ss.at[i], o_rs.at[i], target),
            remote(stat_send.at[hf, d - 1], stat_recv.at[hf, slot], st_ss.at[i], st_rs.at[i], target),
        )

    def project(hf):
        for slot in range(1, NZ):
            for cp in o_in[hf, slot]:
                cp.wait_recv()
        zeros = jnp.zeros((120, tok_h), jnp.float32)
        levels = [jnp.transpose(jnp.concatenate([stat_recv[hf, i], zeros], axis=0)) for i in range(NZ)]
        top = functools.reduce(jnp.maximum, levels)
        shares = [jnp.exp2(v - top) for v in levels]
        whole = functools.reduce(jnp.add, shares)
        shares = [v / whole for v in shares]
        for g in range(GROUP):
            at = slice(g * 128, (g + 1) * 128)
            mixed = shares[0][:, g:g + 1] * o_own[hf, :, at]
            for i in range(1, NZ):
                mixed += shares[i][:, g:g + 1] * o_recv[hf, i - 1, :, at].astype(jnp.float32)
            attended[hf, :, at] = mixed.astype(jnp.bfloat16)
        for ci in range(n_cols // CHUNK):
            at = slice(ci * CHUNK, (ci + 1) * CHUNK)
            part[hf, :, at] = jnp.dot(
                attended[hf], w_v[:, at], preferred_element_type=jnp.float32
            ).astype(jnp.bfloat16)
            for d in range(1, nx):
                i = (hf * (n_cols // CHUNK) + ci) * nx + d
                p_in[hf, ci, d] = remote(
                    part.at[hf, own_rows(at_x(d), NL * part_rows), at], x_recv.at[hf, d - 1, :, at],
                    p_ss.at[i], p_rs.at[i], dev(seq, at_x(d) * NL + zl))

    def exchange(hf):
        for ci in range(n_cols // CHUNK):
            at = slice(ci * CHUNK, (ci + 1) * CHUNK)
            total = part[hf, own_rows(x, NL * part_rows), at].astype(jnp.float32)
            for d in range(1, nx):
                p_in[hf, ci, d].wait_recv()
                total += x_recv[hf, d - 1, :, at].astype(jnp.float32)
            summed[hf, :, at] = total
            z_send[hf, :, at] = summed[hf, own_rows(1 - zl, part_rows), at].astype(jnp.bfloat16)
            i = hf * (n_cols // CHUNK) + ci
            e_in[hf, ci] = remote(z_send.at[hf, :, at], z_recv.at[hf, :, at], e_ss.at[i], e_rs.at[i],
                                  dev(seq, x * NL + 1 - zl))

    def finish(hf, step):
        here = slice(hf * part_rows, (hf + 1) * part_rows)
        for ci in range(n_cols // CHUNK):
            at = slice(ci * CHUNK, (ci + 1) * CHUNK)
            e_in[hf, ci].wait_recv()
            total = summed[hf, own_rows(zl, part_rows), at] + z_recv[hf, :, at].astype(jnp.float32)
            gate = gate_v[pl.ds(step, 1), at]
            out_ref[here, at] = (res_v[here, at].astype(jnp.float32) + gate * total).astype(out_ref.dtype)

    load_tile(0)

    def only_first(jc, carry):
        first(jc, tiles[0][1], 0)
        return carry

    lax.fori_loop(0, n_chunks, only_first, 0)
    close_first()
    for t, (hf, d) in enumerate(tiles):
        more = t + 1 < len(tiles)
        if more:
            load_tile(t + 1)

        def both(jc, carry):
            second(jc, d, t % 2)
            if more:
                first(jc, tiles[t + 1][1], 1 - t % 2)
            return carry

        lax.fori_loop(0, n_chunks, both, 0)
        close_second(hf, d)
        if more:
            close_first()
        if t == len(tiles) - 2:
            local[3].wait()
            project(0)
    project(1)
    exchange(0)
    exchange(1)
    local[4].wait()
    local[5].wait()
    step = steps_ref[map_ref[seq]]
    finish(0, step)
    finish(1, step)
    for cp in sends:
        cp.wait_send()


def per_device(ny, nh, query, key, value, residual, out_weight, gate_table, noise_steps, segment_mask, segment_map):
    rows, n_cols = query.shape
    tok = rows * nh
    half_rows, tok_h = rows // HALVES, tok // HALVES
    rows_t = GROUP * tok_h
    n_keys = 2 * ny * tok
    bf, f32 = jnp.bfloat16, jnp.float32
    dma = lambda n: pltpu.SemaphoreType.DMA((n,))
    n_p = n_cols // CHUNK * HALVES
    nx = nh // NL
    hbm = pl.BlockSpec(memory_space=pl.ANY)
    smem = pl.BlockSpec(memory_space=pltpu.SMEM)
    ring = [dma(2 * ny)] * 6
    return pl.pallas_call(
        functools.partial(kernel, ny, nh, rows),
        out_shape=jax.ShapeDtypeStruct(residual.shape, residual.dtype),
        in_specs=[hbm] * 6 + [smem] * 3,
        out_specs=pl.BlockSpec(memory_space=pltpu.VMEM),
        scratch_shapes=[
            pltpu.VMEM((n_keys, 384), bf),
            pltpu.VMEM((NZ, HALVES, tok_h, GW), bf),
            pltpu.VMEM((2, rows_t, 128), bf),
            pltpu.VMEM((2, rows_t, n_keys), f32),
            pltpu.VMEM((rows_t, 128), f32),
            pltpu.VMEM((rows_t, 128), f32),
            pltpu.VMEM((rows_t, 256), f32),
            pltpu.VMEM((HALVES, NZ - 1, 8, tok_h), f32),
            pltpu.VMEM((HALVES, NZ, 8, tok_h), f32),
            pltpu.VMEM((HALVES, tok_h, GW), f32),
            pltpu.VMEM((HALVES, NZ - 1, tok_h, GW), bf),
            pltpu.VMEM((HALVES, NZ - 1, tok_h, GW), bf),
            pltpu.VMEM((HALVES, tok_h, GW), bf),
            pltpu.VMEM(out_weight.shape, bf),
            pltpu.VMEM(gate_table.shape, f32),
            pltpu.VMEM(residual.shape, bf),
            pltpu.VMEM((HALVES, tok_h, n_cols), bf),
            pltpu.VMEM((HALVES, nx - 1, NL * half_rows, n_cols), bf),
            pltpu.VMEM((HALVES, NL * half_rows, n_cols), f32),
            pltpu.VMEM((HALVES, half_rows, n_cols), bf),
            pltpu.VMEM((HALVES, half_rows, n_cols), bf),
            pltpu.SMEM((NZ * 2 * ny,), f32),
            dma(nh), dma(nh), dma(nh), dma(nh), dma(nh), dma(nh), dma(HALVES * NZ), dma(HALVES * NZ),
            *ring,
            dma(HALVES * NZ), dma(HALVES * NZ), dma(HALVES * NZ), dma(HALVES * NZ),
            dma(n_p * nx), dma(n_p * nx), dma(n_p), dma(n_p), dma(6),
        ],
        compiler_params=pltpu.CompilerParams(
            collective_id=0, has_side_effects=True, vmem_limit_bytes=56 * 2**20
        ),
        name="segment_attention",
    )(
        query.reshape(HALVES, half_rows, n_cols), key, value, residual, out_weight, gate_table,
        noise_steps, segment_mask, segment_map,
    )


def solution(mesh):
    nh = mesh.shape["head"]
    ny = mesh.shape["seq"] // (NZ * NC)
    rows = P(("seq", "head"), None)
    return jax.shard_map(
        functools.partial(per_device, ny, nh),
        mesh=mesh,
        in_specs=(rows, rows, rows, rows, P("head", None), P(), P(), P(), P()),
        out_specs=rows,
        check_vma=False,
    )
```

time: 105 us -> 84.8 us (0.81)
  Pallas kernels: 103 us -> 81.7 us
    pallas_call x1, Pallas kernels: 103 us -> 81.7 us  [per_device(): pl.pallas_call(functools.partial(kernel, ny, nh, rows), out_shape=jax.Sha...]
where the time goes in v2:
time: 84.8 us; the launch traced here: 83.3 us
  Pallas kernels  81.7 us (96%)
  local copies, waits for them, and re-layouts  1.62 us (2%)
    pallas_call x1, Pallas kernels, per_device(): pl.pallas_call(functools.partial(kernel, ny, nh, rows), out_shape=jax.Sha...  81.7 us

profile of v2, /device:TPU:6, one launch (start us, length us, event | category | flops | bytes accessed | tf_op | source)
XLA Modules:
  0.0 83.3 jit_solution(10049040081844719464)
XLA Ops:
  0.0 81.7 %segment_attention.1 = bf16[32,3072]{1,0:T(8,128)(2,1)} custom-call(bf16[2,16,3072]{2,1,0:T(8,128)(2,1)} %bitcast.1, bf16[32,1024]{1,0:T(8,128)(2,1)} %k_hbm.1, bf16[32,1024]{1,0:T(8,128)(2,1)} %v_hbm.1, bf16[32,3072]{1,0:T(8,128)(2,1)} %res_hbm.1, bf16[384,3072]{1,0:T(8,128)(2,1)} %w_hbm.1, f32[64,3072]{1,0:T(8,128)} %gate_hbm.1, s32[8]{0:T(128)} %steps_ref.1, ...), custom_call_target="tpu_custom_call" | custom-call | tf_op jit(solution)/shard_map/segment_attention/pallas_call | solution.py:360
  81.7 1.6 %copy.11 = bf16[32,3072]{1,0:T(8,128)(2,1)} copy(bf16[32,3072]{1,0:T(8,128)(2,1)} %segment_attention.1) | data formatting | bytes 393216

commit v3 on v2

v3 whole, which is shorter than its diff:
```python
import functools

import jax
import jax.numpy as jnp
from jax import lax
from jax.experimental import pallas as pl
from jax.experimental.pallas import tpu as pltpu
from jax.sharding import PartitionSpec as P

HEAD_DIM = 128
GROUP = 3
GW = GROUP * HEAD_DIM
NZ = 4
NC = 2
NL = 2
Z_FIRST = ((1, 1), (1, 2))
AHEAD = 3
HALVES = 2
MASKED = -1e30
FLOOR = -1e20
SCALE = 1.4426950408889634 / HEAD_DIM**0.5
MESH = pl.DeviceIdType.MESH
CHUNK = 1024


def nt_dot(a, b):
    return lax.dot_general(a, b, (((1,), (1,)), ((), ())), preferred_element_type=jnp.float32)


def kernel(
    ny, nh, rows,
    q_hbm, k_hbm, v_hbm, res_hbm, w_hbm, gate_hbm, steps_ref, mask_ref, map_ref,
    out_ref,
    keys, values, q_all, q_tile, scores, mx_acc, mx, acc, stat_send, stat_recv, o_own, o_send, o_recv,
    attended, w_v, gate_v, res_v, part, x_recv, summed, z_send, z_recv, zf_recv, xs_send, xs_recv, bias,
    k_ss, k_rs, v_ss, v_rs, q_ss, q_rs, z_ss, z_rs, right_ss, right_rs, left_ss, left_rs,
    sib_ss, sib_rs, o_ss, o_rs, st_ss, st_rs, p_ss, p_rs, e_ss, e_rs, loc,
):
    seq = lax.axis_index("seq")
    head = lax.axis_index("head")
    core = lax.rem(seq, NC)
    zh = lax.rem(seq // NC, NZ)
    y = seq // (NC * NZ)
    nx = nh // NL
    x = head // NL
    zl = lax.rem(head, NL)
    tok = rows * nh
    part_rows = rows // HALVES
    tok_h = tok // HALVES
    n_slots = 2 * ny
    half = ny // 2
    near = [0, 1] + [r for s in range(1, half) for r in (ny - s, s + 1)]
    spot = {r: i for i, r in enumerate(near)}

    def place(py, pz, pc):
        return (py * NZ + pz) * NC + pc

    def at_head(d):
        return lax.rem(head + d, nh)

    def at_x(d):
        return lax.rem(x + d, nx)

    def at_z(d):
        return lax.rem(zh + d, NZ)

    def at_y(d):
        return lax.rem(y + d + ny, ny)

    def dev(s, h):
        return {"seq": s, "head": h}

    other = place(y, zh, 1 - core)
    right = place(at_y(1), zh, core)
    left = place(at_y(-1), zh, core)
    peers = [dev(seq, at_head(d)) for d in range(1, nh)]
    peers += [dev(place(y, at_z(d), core), head) for d in range(1, NZ)]
    peers += [dev(other, head), dev(right, head), dev(left, head)]

    barrier = pltpu.get_barrier_semaphore()
    for target in peers:
        pl.semaphore_signal(barrier, inc=1, device_id=target, device_id_type=MESH)

    def cols(h, width):
        return pl.ds(pl.multiple_of(h * width, HEAD_DIM), width)

    def own_rows(h, count):
        return pl.ds(pl.multiple_of(h * count, count), count)

    local = [
        pltpu.make_async_copy(k_hbm.at[:, cols(head, HEAD_DIM)], keys.at[own_rows(head, rows)], loc.at[0]),
        pltpu.make_async_copy(v_hbm.at[:, cols(head, HEAD_DIM)], values.at[own_rows(head, rows)], loc.at[1]),
        pltpu.make_async_copy(q_hbm.at[:, :, cols(head, GW)], q_all.at[0, :, own_rows(head, part_rows)], loc.at[2]),
        pltpu.make_async_copy(w_hbm, w_v, loc.at[3]),
        pltpu.make_async_copy(gate_hbm, gate_v, loc.at[4]),
        pltpu.make_async_copy(res_hbm, res_v, loc.at[5]),
    ]
    for cp in local[:3]:
        cp.start()

    q_segs = [map_ref[place(y, at_z(d), core)] for d in range(NZ)]
    for j in range(n_slots):
        k_seg = map_ref[place(at_y(near[j // 2]), zh, core if j % 2 == 0 else 1 - core)]
        for d in range(NZ):
            bias[d * n_slots + j] = jnp.where(mask_ref[q_segs[d], k_seg] > 0, 0.0, MASKED).astype(jnp.float32)

    pl.semaphore_wait(barrier, len(peers))

    sends = []

    def remote(src, dst, ss, rs, target):
        cp = pltpu.make_async_remote_copy(
            src_ref=src, dst_ref=dst, send_sem=ss, recv_sem=rs, device_id=target, device_id_type=MESH
        )
        cp.start()
        sends.append(cp)
        return cp

    kv_in, q_in = [], []
    for d in range(1, nh):
        target = dev(seq, at_head(d))
        kv_in.append(remote(k_hbm.at[:, cols(at_head(d), HEAD_DIM)], keys.at[own_rows(head, rows)],
                            k_ss.at[d], k_rs.at[d], target))
        kv_in.append(remote(v_hbm.at[:, cols(at_head(d), HEAD_DIM)], values.at[own_rows(head, rows)],
                            v_ss.at[d], v_rs.at[d], target))
    for d in range(1, nh):
        q_in.append(remote(q_hbm.at[:, :, cols(at_head(d), GW)], q_all.at[0, :, own_rows(head, part_rows)],
                           q_ss.at[d], q_rs.at[d], dev(seq, at_head(d))))

    z_in = {}

    def send_queries():
        local[2].wait()
        for cp in q_in:
            cp.wait_recv()
        for hf in range(HALVES):
            for dz in (1, 3, 2):
                slot = NZ - dz
                i = hf * NZ + dz
                z_in[hf, slot] = remote(q_all.at[0, hf], q_all.at[slot, hf], z_ss.at[i], z_rs.at[i],
                                        dev(place(y, at_z(dz), core), head))
        for cp in local[3:]:
            cp.start()

    local[0].wait()
    local[1].wait()
    for cp in kv_in:
        cp.wait_recv()

    def block(r, c, held):
        return held.at[pl.ds((spot[r] * 2 + c) * tok, tok)]

    n_chunks = n_slots * tok // CHUNK
    per = CHUNK // tok
    rows_t = GROUP * tok_h

    def key_rows_of(jc):
        return pl.ds(pl.multiple_of(jc * CHUNK, CHUNK), CHUNK)

    def first(jc, d, buf):
        s = nt_dot(q_tile[buf], keys[key_rows_of(jc)])
        scores[buf, :, key_rows_of(jc)] = s
        m = mx_acc[buf]
        for b in range(per):
            off = bias[d * n_slots + jc * per + b]
            for e in range(tok // 128):
                at = b * tok + e * 128
                m = jnp.maximum(m, s[:, at:at + 128] + off)
        mx_acc[buf] = m

    def second(jc, d, buf):
        m = mx[buf]
        pieces = []
        s = scores[buf, :, key_rows_of(jc)]
        for b in range(per):
            shift = (bias[d * n_slots + jc * per + b] - m) * SCALE
            for e in range(tok // 128):
                at = b * tok + e * 128
                pieces.append(jnp.exp2(s[:, at:at + 128] * SCALE + shift).astype(jnp.bfloat16))
        p = jnp.concatenate(pieces, axis=1)
        beside = jnp.concatenate([values[key_rows_of(jc)], jnp.ones((CHUNK, 128), jnp.bfloat16)], axis=1)
        acc[...] += jnp.dot(p, beside, preferred_element_type=jnp.float32)

    def open_first(buf):
        mx_acc[buf] = jnp.full((rows_t, 128), FLOOR, jnp.float32)

    def close_first(buf):
        mx[buf] = jnp.broadcast_to(jnp.max(mx_acc[buf], axis=1, keepdims=True), (rows_t, 128))

    tiles = [(hf, d) for hf in range(HALVES) for d in (1, 3, 2, 0)]
    lane = lax.broadcasted_iota(jnp.int32, (tok_h, 128), 1)

    def load_tile(t):
        hf, d = tiles[t]
        if d:
            z_in[hf, d].wait_recv()
        for g in range(GROUP):
            q_tile[t % AHEAD, g * tok_h:(g + 1) * tok_h] = q_all[d, hf, :, g * 128:(g + 1) * 128]
        open_first(t % AHEAD)

    def early(lo, hi):
        for t in range(AHEAD - 1):
            def step_early(jc, carry, t=t):
                first(jc, tiles[t][1], t)
                return carry

            lax.fori_loop(lo, hi, step_early, 0)

    sib = {}
    parts = (keys, values)

    def pass_on(r, i):
        sib[r, i] = remote(block(r, 0, parts[i]), block(r, 1, parts[i]),
                           sib_ss.at[2 * r + i], sib_rs.at[2 * r + i], dev(other, head))

    waited = []

    def arrived(count):
        for r in near[:2 * (count - 1)]:
            for i in range(2):
                if (r, i) not in waited:
                    waited.append((r, i))
                    sib[r, i].wait_recv()

    r_in, l_in = {}, {}
    for s in range(half + 1):
        for i in range(2):
            held = parts[i]
            if s and i in r_in:
                r_in.pop(i).wait_recv()
            if s < half - 1 or (s == half - 1 and i == 0):
                r_in[i] = remote(block((ny - s) % ny, 0, held), block((ny - s - 1) % ny, 0, held),
                                 right_ss.at[2 * s + i], right_rs.at[2 * s + i], dev(right, head))
            if s and i in l_in:
                l_in.pop(i).wait_recv()
            if s < half - 1 or (s == half - 1 and i == 1):
                l_in[i] = remote(block(s, 0, held), block(s + 1, 0, held),
                                 left_ss.at[2 * s + i], left_rs.at[2 * s + i], dev(left, head))
            pass_on(s, i)
            if 0 < s < half:
                pass_on(ny - s, i)
        if s == 0:
            send_queries()
        if s == half - 1:
            for t in range(AHEAD - 1):
                load_tile(t)
            arrived(half - 1)
            early(0, half - 2)
    arrived(half)
    early(half - 2, half - 1)
    arrived(half + 1)
    early(half - 1, half)

    n_cols = w_v.shape[1]
    n_p = n_cols // CHUNK
    o_in, p_in, e_in = {}, {}, {}

    def close_second(hf, d, buf):
        total = jnp.maximum(acc[:, 128:256], 1e-30)
        value = acc[:, 0:128] / total
        level = mx[buf] * SCALE + jnp.log2(total)
        stat = level[0:tok_h]
        for g in range(1, GROUP):
            stat = jnp.where(lane == g, level[g * tok_h:(g + 1) * tok_h], stat)
        stat = jnp.transpose(stat)[0:8]
        for g in range(GROUP):
            piece = value[g * tok_h:(g + 1) * tok_h]
            if d == 0:
                o_own[hf, :, g * 128:(g + 1) * 128] = piece
            else:
                o_send[hf, d - 1, :, g * 128:(g + 1) * 128] = piece.astype(jnp.bfloat16)
        if d == 0:
            stat_recv[hf, 0] = stat
            return
        slot = NZ - d
        stat_send[hf, d - 1] = stat
        target = dev(place(y, at_z(d), core), head)
        i = hf * NZ + d
        o_in[hf, slot] = (
            remote(o_send.at[hf, d - 1], o_recv.at[hf, slot - 1], o_ss.at[i], o_rs.at[i], target),
            remote(stat_send.at[hf, d - 1], stat_recv.at[hf, slot], st_ss.at[i], st_rs.at[i], target),
        )

    def project(hf):
        for slot in range(1, NZ):
            for cp in o_in[hf, slot]:
                cp.wait_recv()
        zeros = jnp.zeros((120, tok_h), jnp.float32)
        levels = [jnp.transpose(jnp.concatenate([stat_recv[hf, i], zeros], axis=0)) for i in range(NZ)]
        top = functools.reduce(jnp.maximum, levels)
        shares = [jnp.exp2(v - top) for v in levels]
        whole = functools.reduce(jnp.add, shares)
        shares = [v / whole for v in shares]
        for g in range(GROUP):
            at = slice(g * 128, (g + 1) * 128)
            mixed = shares[0][:, g:g + 1] * o_own[hf, :, at]
            for i in range(1, NZ):
                mixed += shares[i][:, g:g + 1] * o_recv[hf, i - 1, :, at].astype(jnp.float32)
            attended[hf, :, at] = mixed.astype(jnp.bfloat16)
        for ci in (1, 2, 0):
            at = slice(ci * CHUNK, (ci + 1) * CHUNK)
            product = jnp.dot(attended[hf], w_v[:, at], preferred_element_type=jnp.float32)
            part[hf, :, :, :, at] = product.astype(jnp.bfloat16).reshape(nx, NL, part_rows, CHUNK)
            if (hf, ci) in Z_FIRST:
                i = hf * n_p + ci
                e_in[hf, ci] = remote(part.at[hf, :, 1 - zl, :, at], zf_recv.at[:, :, at],
                                      e_ss.at[i], e_rs.at[i], dev(seq, x * NL + 1 - zl))
                continue
            for d in range(1, nx):
                i = (hf * n_p + ci) * nx + d
                p_in[hf, ci, d] = remote(part.at[hf, at_x(d), :, :, at], x_recv.at[hf, d - 1, :, :, at],
                                         p_ss.at[i], p_rs.at[i], dev(seq, at_x(d) * NL + zl))

    def exchange(hf, ci):
        at = slice(ci * CHUNK, (ci + 1) * CHUNK)
        if (hf, ci) in Z_FIRST:
            e_in[hf, ci].wait_recv()
            for d in range(nx):
                total = part[hf, at_x(d), zl, :, at].astype(jnp.float32) + zf_recv[at_x(d), :, at].astype(jnp.float32)
                if d == 0:
                    summed[hf, 0, :, at] = total
                    continue
                xs_send[d - 1, :, at] = total.astype(jnp.bfloat16)
                i = (hf * n_p + ci) * nx + d
                p_in[hf, ci, d] = remote(xs_send.at[d - 1, :, at], xs_recv.at[d - 1, :, at],
                                         p_ss.at[i], p_rs.at[i], dev(seq, at_x(d) * NL + zl))
            return
        total = part[hf, x, :, :, at].astype(jnp.float32)
        for d in range(1, nx):
            p_in[hf, ci, d].wait_recv()
            total += x_recv[hf, d - 1, :, :, at].astype(jnp.float32)
        summed[hf, :, :, at] = total
        z_send[hf, :, at] = summed[hf, 1 - zl, :, at].astype(jnp.bfloat16)
        i = hf * n_p + ci
        e_in[hf, ci] = remote(z_send.at[hf, :, at], z_recv.at[hf, :, at], e_ss.at[i], e_rs.at[i],
                              dev(seq, x * NL + 1 - zl))

    def finish(hf, ci, step):
        here = slice(hf * part_rows, (hf + 1) * part_rows)
        at = slice(ci * CHUNK, (ci + 1) * CHUNK)
        if (hf, ci) in Z_FIRST:
            total = summed[hf, 0, :, at]
            for d in range(1, nx):
                p_in[hf, ci, d].wait_recv()
                total += xs_recv[d - 1, :, at].astype(jnp.float32)
        else:
            e_in[hf, ci].wait_recv()
            total = summed[hf, zl, :, at] + z_recv[hf, :, at].astype(jnp.float32)
        gate = gate_v[pl.ds(step, 1), at]
        out_ref[here, at] = (res_v[here, at].astype(jnp.float32) + gate * total).astype(out_ref.dtype)

    for t in range(AHEAD - 1):
        close_first(t)
    for t, (hf, d) in enumerate(tiles):
        ahead = t + AHEAD - 1
        more = ahead < len(tiles)
        if more:
            load_tile(ahead)
        acc[...] = jnp.zeros((rows_t, 256), jnp.float32)

        def both(jc, carry):
            second(jc, d, t % AHEAD)
            if more:
                first(jc, tiles[ahead][1], ahead % AHEAD)
            return carry

        lax.fori_loop(0, n_chunks, both, 0)
        close_second(hf, d, t % AHEAD)
        if more:
            close_first(ahead % AHEAD)
        if t == len(tiles) - 2:
            local[3].wait()
            project(0)
    project(1)
    later = [(1, ci) for ci in (1, 2, 0)]
    for ci in range(n_p):
        exchange(0, ci)
    for hf, ci in later:
        exchange(hf, ci)
    local[4].wait()
    local[5].wait()
    step = steps_ref[map_ref[seq]]
    for ci in range(n_p):
        finish(0, ci, step)
    for hf, ci in later:
        finish(hf, ci, step)
    for cp in sends:
        cp.wait_send()


def per_device(ny, nh, query, key, value, residual, out_weight, gate_table, noise_steps, segment_mask, segment_map):
    rows, n_cols = query.shape
    tok = rows * nh
    half_rows, tok_h = rows // HALVES, tok // HALVES
    rows_t = GROUP * tok_h
    n_keys = 2 * ny * tok
    bf, f32 = jnp.bfloat16, jnp.float32
    dma = lambda n: pltpu.SemaphoreType.DMA((n,))
    n_p = n_cols // CHUNK * HALVES
    nx = nh // NL
    hbm = pl.BlockSpec(memory_space=pl.ANY)
    smem = pl.BlockSpec(memory_space=pltpu.SMEM)
    ring = [dma(2 * ny)] * 6
    return pl.pallas_call(
        functools.partial(kernel, ny, nh, rows),
        out_shape=jax.ShapeDtypeStruct(residual.shape, residual.dtype),
        in_specs=[hbm] * 6 + [smem] * 3,
        out_specs=pl.BlockSpec(memory_space=pltpu.VMEM),
        scratch_shapes=[
            pltpu.VMEM((n_keys, HEAD_DIM), bf),
            pltpu.VMEM((n_keys, HEAD_DIM), bf),
            pltpu.VMEM((NZ, HALVES, tok_h, GW), bf),
            pltpu.VMEM((AHEAD, rows_t, 128), bf),
            pltpu.VMEM((AHEAD, rows_t, n_keys), f32),
            pltpu.VMEM((AHEAD, rows_t, 128), f32),
            pltpu.VMEM((AHEAD, rows_t, 128), f32),
            pltpu.VMEM((rows_t, 256), f32),
            pltpu.VMEM((HALVES, NZ - 1, 8, tok_h), f32),
            pltpu.VMEM((HALVES, NZ, 8, tok_h), f32),
            pltpu.VMEM((HALVES, tok_h, GW), f32),
            pltpu.VMEM((HALVES, NZ - 1, tok_h, GW), bf),
            pltpu.VMEM((HALVES, NZ - 1, tok_h, GW), bf),
            pltpu.VMEM((HALVES, tok_h, GW), bf),
            pltpu.VMEM(out_weight.shape, bf),
            pltpu.VMEM(gate_table.shape, f32),
            pltpu.VMEM(residual.shape, bf),
            pltpu.VMEM((HALVES, nx, NL, half_rows, n_cols), bf),
            pltpu.VMEM((HALVES, nx - 1, NL, half_rows, n_cols), bf),
            pltpu.VMEM((HALVES, NL, half_rows, n_cols), f32),
            pltpu.VMEM((HALVES, half_rows, n_cols), bf),
            pltpu.VMEM((HALVES, half_rows, n_cols), bf),
            pltpu.VMEM((nx, half_rows, n_cols), bf),
            pltpu.VMEM((nx - 1, half_rows, n_cols), bf),
            pltpu.VMEM((nx - 1, half_rows, n_cols), bf),
            pltpu.SMEM((NZ * 2 * ny,), f32),
            dma(nh), dma(nh), dma(nh), dma(nh), dma(nh), dma(nh), dma(HALVES * NZ), dma(HALVES * NZ),
            *ring,
            dma(HALVES * NZ), dma(HALVES * NZ), dma(HALVES * NZ), dma(HALVES * NZ),
            dma(n_p * nx), dma(n_p * nx), dma(n_p), dma(n_p), dma(6),
        ],
        compiler_params=pltpu.CompilerParams(
            collective_id=0, has_side_effects=True, vmem_limit_bytes=56 * 2**20
        ),
        name="segment_attention",
    )(
        query.reshape(HALVES, half_rows, n_cols), key, value, residual, out_weight, gate_table,
        noise_steps, segment_mask, segment_map,
    )


def solution(mesh):
    nh = mesh.shape["head"]
    ny = mesh.shape["seq"] // (NZ * NC)
    rows = P(("seq", "head"), None)
    return jax.shard_map(
        functools.partial(per_device, ny, nh),
        mesh=mesh,
        in_specs=(rows, rows, rows, rows, P("head", None), P(), P(), P(), P()),
        out_specs=rows,
        check_vma=False,
    )
```

time: 84.8 us -> 82.5 us (0.973)
  Pallas kernels: 81.7 us -> 79.8 us
    pallas_call x1, Pallas kernels: 81.7 us -> 79.8 us  [per_device(): pl.pallas_call(functools.partial(kernel, ny, nh, rows), out_shape=jax.Sha...]
where the time goes in v3:
time: 82.5 us; the launch traced here: 81.4 us
  Pallas kernels  79.8 us (97%)
  local copies, waits for them, and re-layouts  1.62 us (2%)
    pallas_call x1, Pallas kernels, per_device(): pl.pallas_call(functools.partial(kernel, ny, nh, rows), out_shape=jax.Sha...  79.8 us

profile of v3, /device:TPU:6, one launch (start us, length us, event | category | flops | bytes accessed | tf_op | source)
XLA Modules:
  0.0 81.4 jit_solution(8519497218469760983)
XLA Ops:
  0.0 79.8 %segment_attention.1 = bf16[32,3072]{1,0:T(8,128)(2,1)} custom-call(bf16[2,16,3072]{2,1,0:T(8,128)(2,1)} %bitcast.1, bf16[32,1024]{1,0:T(8,128)(2,1)} %k_hbm.1, bf16[32,1024]{1,0:T(8,128)(2,1)} %v_hbm.1, bf16[32,3072]{1,0:T(8,128)(2,1)} %res_hbm.1, bf16[384,3072]{1,0:T(8,128)(2,1)} %w_hbm.1, f32[64,3072]{1,0:T(8,128)} %gate_hbm.1, s32[8]{0:T(128)} %steps_ref.1, ...), custom_call_target="tpu_custom_call" | custom-call | tf_op jit(solution)/shard_map/segment_attention/pallas_call | solution.py:404
  79.8 1.6 %copy.11 = bf16[32,3072]{1,0:T(8,128)(2,1)} copy(bf16[32,3072]{1,0:T(8,128)(2,1)} %segment_attention.1) | data formatting | bytes 393216

commit v4 on v3

--- a/solution.py
+++ b/solution.py
@@ -33,7 +33,7 @@
     out_ref,
     keys, values, q_all, q_tile, scores, mx_acc, mx, acc, stat_send, stat_recv, o_own, o_send, o_recv,
     attended, w_v, gate_v, res_v, part, x_recv, summed, z_send, z_recv, zf_recv, xs_send, xs_recv, bias,
-    k_ss, k_rs, v_ss, v_rs, q_ss, q_rs, z_ss, z_rs, right_ss, right_rs, left_ss, left_rs,
+    k_ss, k_rs, v_ss, v_rs, q_ss, q_rs, z_ss, z_rs, ring_ss, ring_rs,
     sib_ss, sib_rs, o_ss, o_rs, st_ss, st_rs, p_ss, p_rs, e_ss, e_rs, loc,
 ):
     seq = lax.axis_index("seq")
@@ -75,7 +75,8 @@
     left = place(at_y(-1), zh, core)
     peers = [dev(seq, at_head(d)) for d in range(1, nh)]
     peers += [dev(place(y, at_z(d), core), head) for d in range(1, NZ)]
-    peers += [dev(other, head), dev(right, head), dev(left, head)]
+    right2, left2 = place(at_y(2), zh, core), place(at_y(-2), zh, core)
+    peers += [dev(other, head)] + [dev(p, head) for p in (right, left, right2, left2)]
 
     barrier = pltpu.get_barrier_semaphore()
     for target in peers:
@@ -187,7 +188,7 @@
     def close_first(buf):
         mx[buf] = jnp.broadcast_to(jnp.max(mx_acc[buf], axis=1, keepdims=True), (rows_t, 128))
 
-    tiles = [(hf, d) for hf in range(HALVES) for d in (1, 3, 2, 0)]
+    tiles = [(hf, d) for hf in range(HALVES) for d in (1, 3, 2)] + [(hf, 0) for hf in range(HALVES)]
     lane = lax.broadcasted_iota(jnp.int32, (tok_h, 128), 1)
 
     def load_tile(t):
@@ -222,30 +223,43 @@
                     waited.append((r, i))
                     sib[r, i].wait_recv()
 
-    r_in, l_in = {}, {}
-    for s in range(half + 1):
+    ring = {}
+
+    def go(r, i, d):
+        to = {1: right, -1: left, 2: right2, -2: left2}[d]
+        at = (r - d) % ny
+        ring[at, i] = remote(block(r, 0, parts[i]), block(at, 0, parts[i]),
+                             ring_ss.at[2 * at + i], ring_rs.at[2 * at + i], dev(to, head))
+
+    for i in range(2):
+        for d in (2, -2):
+            go(0, i, d)
+    for i in range(2):
+        for d in (1, -1):
+            go(0, i, d)
+    send_queries()
+    for i in range(2):
+        pass_on(0, i)
+    for i in range(2):
+        for d in (2, -2):
+            r = -d % ny
+            ring[r, i].wait_recv()
+            go(r, i, d // 2)
+            if (i == 0) == (d > 0):
+                go(r, i, d)
+    for r in (ny - 2, 2, 1, ny - 1):
         for i in range(2):
-            held = parts[i]
-            if s and i in r_in:
-                r_in.pop(i).wait_recv()
-            if s < half - 1 or (s == half - 1 and i == 0):
-                r_in[i] = remote(block((ny - s) % ny, 0, held), block((ny - s - 1) % ny, 0, held),
-                                 right_ss.at[2 * s + i], right_rs.at[2 * s + i], dev(right, head))
-            if s and i in l_in:
-                l_in.pop(i).wait_recv()
-            if s < half - 1 or (s == half - 1 and i == 1):
-                l_in[i] = remote(block(s, 0, held), block(s + 1, 0, held),
-                                 left_ss.at[2 * s + i], left_rs.at[2 * s + i], dev(left, head))
-            pass_on(s, i)
-            if 0 < s < half:
-                pass_on(ny - s, i)
-        if s == 0:
-            send_queries()
-        if s == half - 1:
-            for t in range(AHEAD - 1):
-                load_tile(t)
-            arrived(half - 1)
-            early(0, half - 2)
+            if r in (1, ny - 1):
+                ring[r, i].wait_recv()
+            pass_on(r, i)
+    for t in range(AHEAD - 1):
+        load_tile(t)
+    arrived(half - 1)
+    early(0, half - 2)
+    for r in (ny - 3, 3, half):
+        for i in range(2):
+            ring[r, i].wait_recv()
+            pass_on(r, i)
     arrived(half)
     early(half - 2, half - 1)
     arrived(half + 1)
@@ -400,7 +414,7 @@
     nx = nh // NL
     hbm = pl.BlockSpec(memory_space=pl.ANY)
     smem = pl.BlockSpec(memory_space=pltpu.SMEM)
-    ring = [dma(2 * ny)] * 6
+    ring = [dma(2 * ny)] * 4
     return pl.pallas_call(
         functools.partial(kernel, ny, nh, rows),
         out_shape=jax.ShapeDtypeStruct(residual.shape, residual.dtype),

time: 82.5 us -> 79.2 us (0.960)
  Pallas kernels: 79.8 us -> 76.1 us
    pallas_call x1, Pallas kernels: 79.8 us -> 76.1 us  [per_device(): pl.pallas_call(functools.partial(kernel, ny, nh, rows), out_shape=jax.Sha...]
where the time goes in v4:
time: 79.2 us; the launch traced here: 77.7 us
  Pallas kernels  76.1 us (96%)
  local copies, waits for them, and re-layouts  1.62 us (2%)
    pallas_call x1, Pallas kernels, per_device(): pl.pallas_call(functools.partial(kernel, ny, nh, rows), out_shape=jax.Sha...  76.1 us
    unnamed x1, local copies, waits for them, and re-layouts  1.62 us

profile of v4, /device:TPU:6, one launch (start us, length us, event | category | flops | bytes accessed | tf_op | source)
XLA Modules:
  0.0 77.7 jit_solution(595245350451762181)
XLA Ops:
  0.0 76.1 %segment_attention.1 = bf16[32,3072]{1,0:T(8,128)(2,1)} custom-call(bf16[2,16,3072]{2,1,0:T(8,128)(2,1)} %bitcast.1, bf16[32,1024]{1,0:T(8,128)(2,1)} %k_hbm.1, bf16[32,1024]{1,0:T(8,128)(2,1)} %v_hbm.1, bf16[32,3072]{1,0:T(8,128)(2,1)} %res_hbm.1, bf16[384,3072]{1,0:T(8,128)(2,1)} %w_hbm.1, f32[64,3072]{1,0:T(8,128)} %gate_hbm.1, s32[8]{0:T(128)} %steps_ref.1, ...), custom_call_target="tpu_custom_call" | custom-call | tf_op jit(solution)/shard_map/segment_attention/pallas_call | solution.py:418
  76.1 1.6 %copy.11 = bf16[32,3072]{1,0:T(8,128)(2,1)} copy(bf16[32,3072]{1,0:T(8,128)(2,1)} %segment_attention.1) | data formatting | bytes 393216
